TPU v7x, 128 devices: a whole 4x4x4 slice. The times are simulated.
128 devices in a mesh: seq: 128 (over x, z, y, core).
Axes of the slice: x: 4, y: 4, z: 4, core: 2. Of those that a mesh axis runs over, the one named last changes fastest.
Arguments:
- queries: bfloat16 [16384, 1280], P('seq'), may hold values from -6 to 6
- key_states: bfloat16 [16384, 1280], P('seq'), may hold values from -6 to 6
- value_states: bfloat16 [16384, 1280], P('seq'), may hold values from -6 to 6
- offsets: int32 [2, 16], replicated, may hold values from 0 to 31, as said below
- out_weight: bfloat16 [1280, 1280], replicated, may hold values from -0.15625 to 0.15625
Outputs:
- attended: bfloat16 [16384, 1280], P('seq')
Inputs may be any that keep to these rules, and one draw needn't show every extreme that they name: `offsets`: offsets in row 0 are below 8, those in row 1 below 32.
All inputs are finite; a program needn't handle non-finite values.
Results may differ from a plain program's by a relative error of at most 0.0054.
Values may be sent and summed in bfloat16 or wider, within the bound.
No kernel may reach another device: no remote copies, remote signals or barrier semaphores. Data moves between devices by JAX's collectives and lax.ppermute only.
A program may use at most 128 MiB of HBM per device.

v0:
```python
import functools
import math

import jax
import jax.numpy as jnp
from jax import lax
from jax.experimental import pallas as pl
from jax.experimental.pallas import tpu as pltpu
from jax.sharding import PartitionSpec as P

HEADS = 16
HDIM = 80
SEG1 = 2048
SEGS = 8
ROWS = 128
D2 = 8
D3 = 32
C2 = SEG1 // D2
C3 = SEG1 // D3
ROW_L = HDIM
ROW_M = HDIM + 8
AUG = HDIM + 16
SCALE = math.log2(math.e) / math.sqrt(HDIM)
LOW = -1e30
FLOOR = -1e9
IN_ROOT = (14, 14)
OUT_ROOT = (13, 10)
BF = jnp.bfloat16
F32 = jnp.float32


def listed(root):
    return [(root + n) % HEADS for n in range(HEADS)]


def spot(chip, roots):
    if roots[0] == roots[1]:
        return (chip - roots[0]) % HEADS
    core = lax.rem(lax.axis_index("seq"), 2)
    return lax.rem(chip + HEADS - roots[0] - (roots[1] - roots[0]) * core, HEADS)


def contract0(a, b):
    return lax.dot_general(a, b, (((0,), (0,)), ((), ())), preferred_element_type=F32)


def dot(a, b):
    return jnp.dot(a, b, preferred_element_type=F32)


def iota(shape, dim):
    return lax.broadcasted_iota(jnp.int32, shape, dim)


def onehot(cond):
    return jnp.where(cond, 1.0, 0.0).astype(BF)


def my_offsets(off_ref):
    head = lax.rem(lax.axis_index("seq") // 2, HEADS)
    mine = jnp.where(iota((2, HEADS), 1) == head, off_ref[...], 0)
    both = jnp.sum(mine, axis=1, keepdims=True)
    return both[:1], both[1:]


def picks(off_ref):
    off2, off3 = my_offsets(off_ref)
    tok = iota((1024, 128), 0)
    lane = iota((1024, 128), 1)
    return jnp.concatenate(
        [onehot(tok == lane * D2 + off2), onehot(tok == lane * D3 + off3)], axis=1
    )


def fold(x):
    return jnp.max(x.reshape(x.shape[0] // 8, 8, x.shape[1]), axis=0)


def blocks(ref, first, low, high):
    return jnp.concatenate(
        [ref[spot(s, IN_ROOT), low:high, :] for s in range(first, first + 8)], axis=1
    )


def pack_kernel(q_hbm, k_hbm, v_hbm, out_ref, held, sems):
    copies = [
        pltpu.make_async_copy(ref, held.at[part], sems.at[part])
        for part, ref in enumerate((q_hbm, k_hbm, v_hbm))
    ]
    for copy in copies:
        copy.start()
    half = HEADS * HDIM // 2
    for part in range(3):
        copies[part].wait()
        for n in range(2):
            turned = held[part, :, n * half : (n + 1) * half].T
            for m in range(8):
                slot = spot(8 * n + m, IN_ROOT)
                out_ref[slot, part * HDIM : (part + 1) * HDIM, :] = turned[
                    m * HDIM : (m + 1) * HDIM
                ]


def select_kernel(off_ref, x_ref, kv_ref, all_ref):
    both = jnp.concatenate([blocks(x_ref, 8 * h, 0, 3 * HDIM) for h in range(2)], axis=0)
    got = dot(both, picks(off_ref))
    q0, key0, val0, q1, key1, val1 = [got[n * HDIM : (n + 1) * HDIM] for n in range(6)]
    for n, part in enumerate((key0, key1, val0, val1)):
        kv_ref[n * HDIM : (n + 1) * HDIM, :] = part[:, :128].astype(BF)
    far = key0[:, 128:]
    for n, part in enumerate((key1, val0, val1)):
        far = far + pltpu.roll(part[:, 128:], 32 * (n + 1), 1)
    kv_ref[4 * HDIM :, :] = far.astype(BF)
    for j in range(HEADS):
        all_ref[j] = x_ref[spot(j, IN_ROOT), HDIM:, :]
    all_ref[HEADS, :HDIM, :] = q0[:, :128].astype(BF)
    all_ref[HEADS, HDIM:, :] = q1[:, :128].astype(BF)
    all_ref[HEADS + 1, :HDIM, :] = (q0[:, 128:] + pltpu.roll(q1[:, 128:], 32, 1)).astype(BF)
    all_ref[HEADS + 1, HDIM:, :] = jnp.zeros((HDIM, 128), BF)


def near_kernel(off_ref, x_ref, other_ref, state_ref, spread_ref):
    core = lax.rem(lax.axis_index("seq"), 2)

    def own(s, low, high):
        return x_ref[spot(s, IN_ROOT), low:high, :]

    ones = jnp.ones((16, 256), BF)
    row = iota((256, 256), 0)
    col = iota((256, 256), 1)
    first = col < 128
    last = jnp.where(row < 128, lax.rem(col, 128), 127 + 128 * core)
    diagonal = (row <= jnp.where(first, last, 255), row <= jnp.where(first, -1, last))
    keys = [
        jnp.concatenate([own(s, HDIM, 2 * HDIM), other_ref[s, :HDIM, :]], axis=1).T
        for s in range(HEADS)
    ]

    def score(slot):
        q_t = jnp.concatenate([own(slot + n, 0, HDIM) for n in range(2)], axis=1)
        parts = [dot(keys[n], q_t) for n in range(slot // 8 * 8, slot + 2)]
        for n in range(2):
            parts[n - 2] = jnp.where(diagonal[n], parts[n - 2], LOW)
        return parts

    def weigh(parts):
        top = functools.reduce(jnp.maximum, [fold(p) for p in parts])
        high = jnp.max(top, axis=0, keepdims=True) * SCALE
        return high, [jnp.exp2(p * SCALE - high).astype(BF) for p in parts]

    def gather(slot, high, weights):
        acc = jnp.zeros((AUG, 256), F32)
        for n, part in enumerate(weights):
            s = slot // 8 * 8 + n
            v_t = jnp.concatenate([own(s, 2 * HDIM, 3 * HDIM), other_ref[s, HDIM:, :]], axis=1)
            acc = acc + dot(jnp.concatenate([v_t, ones], axis=0), part)
        cols = slice(slot * 128, (slot + 2) * 128)
        state_ref[:ROW_M, cols] = acc[:ROW_M]
        state_ref[ROW_M:, cols] = jnp.broadcast_to(high, (8, 256))

    order = (6, 14, 4, 12, 2, 10, 0, 8)
    scores = score(order[0])
    waiting = None
    for n, slot in enumerate(order):
        current = scores
        if n + 1 < len(order):
            scores = score(order[n + 1])
        weighed = weigh(current)
        if waiting is not None:
            gather(*waiting)
        waiting = (slot, *weighed)
    gather(*waiting)
    off2, off3 = my_offsets(off_ref)
    lane = iota((128, 1024), 0)
    tok = iota((128, 1024), 1)
    spread_ref[0] = onehot(tok == lane * D2 + off2)
    for half in range(2):
        spread_ref[1 + half] = onehot(tok + half * 1024 == lax.rem(lane, C3) * D3 + off3)


def far_kernel(own, all_ref, *refs):
    pieces, out_ref = refs[:4], refs[-1]
    device = lax.axis_index("seq")
    core = lax.rem(device, 2)
    plane = device // 32

    def attend(width, keys, values, q, slot_rows, cols):
        row = iota((width, q.shape[1]), 0)
        col = iota((width, q.shape[1]), 1)
        if own:
            seen = row <= col
        else:
            seen = row // slot_rows < col // slot_rows + 1 - core
        parts, tops, hides = [], [], []
        for n, k_t in enumerate(keys):
            scores = contract0(k_t, q)[:width]
            if n == 0:
                scores = jnp.where(seen, scores, LOW)
            hide = jnp.where(plane >= n, 0.0, LOW).astype(F32)
            parts.append(scores)
            hides.append(hide)
            tops.append(fold(scores) + hide)
        high = jnp.max(functools.reduce(jnp.maximum, tops), axis=0, keepdims=True) * SCALE
        high = jnp.maximum(high, FLOOR).astype(BF).astype(F32)
        acc = jnp.zeros((AUG, q.shape[1]), F32)
        for v_t, scores, hide in zip(values, parts, hides):
            weights = jnp.exp2(scores * SCALE - (high - hide)).astype(BF)
            if v_t.shape[1] > width:
                zeros = jnp.zeros((v_t.shape[1] - width, q.shape[1]), BF)
                weights = jnp.concatenate([zeros, weights], axis=0)
            ones = jnp.ones((16, v_t.shape[1]), BF)
            acc = acc + dot(jnp.concatenate([v_t, ones], axis=0), weights)
        out_ref[:ROW_M, cols] = acc[:ROW_M]
        out_ref[ROW_M:, cols] = jnp.broadcast_to(high, (8, q.shape[1]))

    def pair(piece, n):
        return jnp.concatenate(
            [piece[n * HDIM : (n + 1) * HDIM, :], piece[(n + 1) * HDIM : (n + 2) * HDIM, :]], axis=1
        )

    keys = [pair(p, 0) for p in pieces]
    values = [pair(p, 2) for p in pieces]
    last = [p[4 * HDIM :, :] for p in pieces]
    q2 = jnp.concatenate([all_ref[HEADS, :HDIM, :], all_ref[HEADS, HDIM:, :]], axis=1)
    attend(C2, keys, values, q2, ROWS // D2, slice(0, C2))
    q3 = all_ref[HEADS + 1, :HDIM, :]
    attend(C3, last, last, q3, ROWS // D3, slice(C2, C2 + 128))


def mix_kernel(off_ref, state_ref, spread_ref, own_ref, other_ref, out_ref):
    off2, off3 = my_offsets(off_ref)
    hi_a, hi_b = own_ref[ROW_M:, :], other_ref[ROW_M:, :]
    high = jnp.maximum(hi_a, hi_b)
    e_a, e_b = jnp.exp2(hi_a - high), jnp.exp2(hi_b - high)
    body = own_ref[:ROW_M, :] * e_a[:1] + other_ref[:ROW_M, :] * e_b[:1]
    top = body.astype(BF)
    rest = (body - top.astype(F32)).astype(BF)
    stat = high.astype(BF)
    top = jnp.concatenate([top, stat], axis=0)
    rest = jnp.concatenate([rest, jnp.zeros_like(stat)], axis=0)
    parts3 = jnp.concatenate([top[:, C2 : C2 + C3], rest[:, C2 : C2 + C3]], axis=1)
    place2 = jnp.concatenate([spread_ref[0], spread_ref[0]], axis=0)
    tok1 = iota((1, 1024), 1)
    for half in range(2):
        near = state_ref[:, half * 1024 : (half + 1) * 1024]
        cols = slice(half * 128, (half + 1) * 128)
        lev2 = dot(jnp.concatenate([top[:, cols], rest[:, cols]], axis=1), place2)
        lev3 = dot(parts3, spread_ref[1 + half])
        hi1 = near[ROW_M : ROW_M + 1]
        hi2 = jnp.where(lax.rem(tok1, D2) == off2, lev2[ROW_M : ROW_M + 1], LOW)
        hi3 = jnp.where(lax.rem(tok1, D3) == off3, lev3[ROW_M : ROW_M + 1], LOW)
        peak = jnp.maximum(jnp.maximum(hi1, hi2), hi3)
        shares = [jnp.exp2(hi - peak) for hi in (hi1, hi2, hi3)]
        levels = (near, lev2, lev3)
        total = sum(e * x[ROW_L : ROW_L + 1] for e, x in zip(shares, levels))
        inv = 1.0 / total
        mixed = sum(x[:HDIM] * (e * inv) for e, x in zip(shares, levels)).astype(BF)
        for s in range(8):
            out_ref[spot(half * 8 + s, OUT_ROOT)] = mixed[:, s * 128 : (s + 1) * 128]


def project_kernel(x_ref, w_ref, out_hbm, held, sems):
    x = jnp.concatenate([x_ref[spot(h, OUT_ROOT)] for h in range(HEADS)], axis=0)
    copies = []
    for n in range(5):
        cols = slice(n * 256, (n + 1) * 256)
        held[:, cols] = contract0(x, w_ref[:, cols]).astype(BF)
        copy = pltpu.make_async_copy(held.at[:, cols], out_hbm.at[:, cols], sems.at[n])
        copy.start()
        copies.append(copy)
    for copy in copies:
        copy.wait()


def call(kernel, out_shapes, vmem, hbm=0, scratch=(), cost=None, out_space=pltpu.VMEM):
    return pl.pallas_call(
        kernel,
        out_shape=out_shapes,
        in_specs=[pl.BlockSpec(memory_space=pltpu.VMEM)] * vmem
        + [pl.BlockSpec(memory_space=pltpu.HBM)] * hbm,
        out_specs=jax.tree.map(lambda _: pl.BlockSpec(memory_space=out_space), out_shapes),
        scratch_shapes=scratch,
        cost_estimate=cost,
        compiler_params=pltpu.CompilerParams(vmem_limit_bytes=40 * 2**20),
    )


def shape(*dims, dtype=BF):
    return jax.ShapeDtypeStruct(dims, dtype)


def on_device(queries, key_states, value_states, offsets, out_weight):
    n_dev = 128
    planes = [
        [[x * 32 + 2 * j + c for j in listed(roots[c])] for x in range(4) for c in range(2)]
        for roots in (IN_ROOT, OUT_ROOT)
    ]
    swap = [(i, i ^ 1) for i in range(n_dev)]
    packed = call(
        pack_kernel,
        shape(HEADS, 3 * HDIM, ROWS),
        0,
        3,
        (pltpu.VMEM((3, ROWS, HEADS * HDIM), BF), pltpu.SemaphoreType.DMA((3,))),
    )(*[pltpu.with_memory_space_constraint(a, pltpu.HBM) for a in (queries, key_states, value_states)])
    mine = lax.all_to_all(packed, "seq", 0, 0, axis_index_groups=planes[0], tiled=True)
    chosen, own_all = call(
        select_kernel, (shape(5 * HDIM, 128), shape(HEADS + 2, 2 * HDIM, ROWS)), 2
    )(offsets, mine)
    other_all = lax.ppermute(own_all, "seq", swap)
    units = [chosen]
    for back in (1, 2, 3):
        pairs = [(i, (i + 32 * back) % n_dev) for i in range(n_dev)]
        units.append(lax.ppermute(chosen, "seq", pairs))
    state, places = call(
        near_kernel,
        (shape(AUG, SEG1, dtype=F32), shape(3, 128, SEG1 // 2)),
        3,
        cost=pl.CostEstimate(flops=6 * 10**9, bytes_accessed=10**7, transcendentals=10**6),
    )(offsets, mine, other_all)
    part = shape(AUG, C2 + 128, dtype=F32)
    sent = call(functools.partial(far_kernel, False), part, 6)(other_all, *units, state)
    kept = call(
        functools.partial(far_kernel, True),
        part,
        6,
        cost=pl.CostEstimate(flops=10**9, bytes_accessed=10**7, transcendentals=10**6),
    )(own_all, *units, state)
    mixed = call(mix_kernel, shape(HEADS, HDIM, ROWS), 5)(
        offsets, state, places, kept, lax.ppermute(sent, "seq", swap)
    )
    home = lax.all_to_all(mixed, "seq", 0, 0, axis_index_groups=planes[1], tiled=True)
    return call(
        project_kernel,
        shape(ROWS, HEADS * HDIM),
        2,
        scratch=(pltpu.VMEM((ROWS, HEADS * HDIM), BF), pltpu.SemaphoreType.DMA((5,))),
        out_space=pltpu.HBM,
    )(home, out_weight)


def solution(mesh):
    placed = (P("seq", None), P("seq", None), P("seq", None), P(), P())
    return jax.shard_map(
        on_device, mesh=mesh, in_specs=placed, out_specs=P("seq", None), check_vma=False
    )
```

profile of v0, /device:TPU:0, one launch (start us, length us, event | category | flops | bytes accessed | tf_op | source)
XLA Modules:
  0.0 49.4 jit_solution(8584583323954418686)
XLA Ops:
  0.0 0.0 copy-start.1
  0.0 1.4 %shard_map.55 = bf16[16,240,128]{2,1,0:T(8,128)(2,1)S(1)} custom-call(bf16[128,1280]{1,0:T(8,128)(2,1)} %q_hbm.1, bf16[128,1280]{1,0:T(8,128)(2,1)} %k_hbm.1, bf16[128,1280]{1,0:T(8,128)(2,1)} %v_hbm.1), custom_call_target="tpu_custom_call" | custom-call | tf_op jit(solution)/shard_map/pallas_call | solution.py:299
  1.4 21.5 %all_to_all.10.x_ref = bf16[16,240,128]{2,1,0:T(8,128)(2,1)S(1)} all-to-all(bf16[16,240,128]{2,1,0:T(8,128)(2,1)S(1)} %shard_map.55), channel_id=1, replica_groups={{28,30,0,2,4,6,8,10,12,14,16,18,20,22,24,26},{29,31,1,3,5,7,9,11,13,15,..., dimensions={0} | all-to-all | bytes 1966080 | tf_op jit(solution)/shard_map/all_to_all | solution.py:306
  23.0 0.0 copy-done.1
  23.0 0.6 %shard_map.56 = (bf16[400,128]{1,0:T(8,128)(2,1)S(1)}, bf16[18,160,128]{2,1,0:T(8,128)(2,1)S(1)}) custom-call(s32[2,16]{1,0:T(2,128)S(1)} %copy-done.1, bf16[16,240,128]{2,1,0:T(8,128)(2,1)S(1)} %all_to_all.10.x_ref), custom_call_target="tpu_custom_call" | custom-call | tf_op jit(solution)/shard_map/pallas_call | solution.py:307
  23.6 0.1 collective-permute-start
  23.7 1.6 %collective-permute-start.1 = (bf16[400,128]{1,0:T(8,128)(2,1)S(1)}, bf16[400,128]{1,0:T(8,128)(2,1)S(1)}, u32[]{:S(2)}, u32[]{:S(2)}) collective-permute-start(bf16[400,128]{1,0:T(8,128)(2,1)S(1)} %get-tuple-element.12.refs_0_), channel_id=1, source_target_pairs={{0,32},{1,33},{2,34},{3,35},{4,36},{5,37},{6,38},{7,39},{8,40},{9,... | collective-permute-start | bytes 307208 | tf_op jit(solution)/shard_map/ppermute | solution.py:314
  25.2 2.7 %collective-permute-start.2 = (bf16[400,128]{1,0:T(8,128)(2,1)S(1)}, bf16[400,128]{1,0:T(8,128)(2,1)S(1)}, u32[]{:S(2)}, u32[]{:S(2)}) collective-permute-start(bf16[400,128]{1,0:T(8,128)(2,1)S(1)} %get-tuple-element.12.refs_0_), channel_id=1, source_target_pairs={{0,64},{1,65},{2,66},{3,67},{4,68},{5,69},{6,70},{7,71},{8,72},{9,... | collective-permute-start | bytes 307208 | tf_op jit(solution)/shard_map/ppermute | solution.py:314
  28.0 1.4 %collective-permute-start.3 = (bf16[400,128]{1,0:T(8,128)(2,1)S(1)}, bf16[400,128]{1,0:T(8,128)(2,1)S(1)}, u32[]{:S(2)}, u32[]{:S(2)}) collective-permute-start(bf16[400,128]{1,0:T(8,128)(2,1)S(1)} %get-tuple-element.12.refs_0_), channel_id=1, source_target_pairs={{0,96},{1,97},{2,98},{3,99},{4,100},{5,101},{6,102},{7,103},{8,104... | collective-permute-start | bytes 307208 | tf_op jit(solution)/shard_map/ppermute | solution.py:314
  29.4 0.0 collective-permute-done.other_ref.all_ref
  29.4 3.3 %shard_map.57 = (f32[96,2048]{1,0:T(8,128)S(1)}, bf16[3,128,1024]{2,1,0:T(8,128)(2,1)S(1)}) custom-call(s32[2,16]{1,0:T(2,128)S(1)} %copy-done.1, bf16[16,240,128]{2,1,0:T(8,128)(2,1)S(1)} %all_to_all.10.x_ref, bf16[18,160,128]{2,1,0:T(8,128)(2,1)S(1)} %collective-permute-done.other_ref.all_ref), custom_call_target="tpu_custom_call" | custom-call | flops 6000000000 | bytes 10000000 | tf_op jit(solution)/shard_map/pallas_call | solution.py:315
  32.8 0.0 collective-permute-done.1.refs_1_
  32.8 0.6 %collective-permute-done.2.refs_2_ = bf16[400,128]{1,0:T(8,128)(2,1)S(1)} collective-permute-done((bf16[400,128]{1,0:T(8,128)(2,1)S(1)}, bf16[400,128]{1,0:T(8,128)(2,1)S(1)}, u32[]{:S(2)}, u32[]{:S(2)}) %collective-permute-start.2) | collective-permute-done | bytes 102432 | tf_op jit(solution)/shard_map/ppermute | solution.py:314
  33.4 0.0 collective-permute-done.3.refs_3_
  33.4 0.8 %shard_map.59 = f32[96,384]{1,0:T(8,128)S(1)} custom-call(bf16[18,160,128]{2,1,0:T(8,128)(2,1)S(1)} %collective-permute-done.other_ref.all_ref, bf16[400,128]{1,0:T(8,128)(2,1)S(1)} %get-tuple-element.12.refs_0_, bf16[400,128]{1,0:T(8,128)(2,1)S(1)} %collective-permute-done.1.refs_1_, bf16[400,128]{1,0:T(8,128)(2,1)S(1)} %collective-permute-done.2.refs_2_, ...), custom_call_target="tpu_custom_call" | custom-call | tf_op jit(solution)/shard_map/pallas_call | solution.py:322
  34.2 0.0 copy-start
  34.2 0.1 collective-permute-start.4
  34.3 0.8 %shard_map.58.own_ref = f32[96,384]{1,0:T(8,128)S(1)} custom-call(bf16[18,160,128]{2,1,0:T(8,128)(2,1)S(1)} %get-tuple-element.9.all_ref, bf16[400,128]{1,0:T(8,128)(2,1)S(1)} %get-tuple-element.12.refs_0_, bf16[400,128]{1,0:T(8,128)(2,1)S(1)} %collective-permute-done.1.refs_1_, bf16[400,128]{1,0:T(8,128)(2,1)S(1)} %collective-permute-done.2.refs_2_, ...), custom_call_target="tpu_custom_call" | custom-call | flops 1000000000 | bytes 10000000 | tf_op jit(solution)/shard_map/pallas_call | solution.py:323
  35.1 0.5 %collective-permute-done.4.other_ref = f32[96,384]{1,0:T(8,128)S(1)} collective-permute-done((f32[96,384]{1,0:T(8,128)S(1)}, f32[96,384]{1,0:T(8,128)S(1)}, u32[]{:S(2)}, u32[]{:S(2)}) %collective-permute-start.4) | collective-permute-done | bytes 147488 | tf_op jit(solution)/shard_map/ppermute | solution.py:330
  35.7 0.5 %shard_map.60 = bf16[16,80,128]{2,1,0:T(8,128)(2,1)S(1)} custom-call(s32[2,16]{1,0:T(2,128)S(1)} %copy-done.1, f32[96,2048]{1,0:T(8,128)S(1)} %get-tuple-element.10.refs_4_.state_ref, bf16[3,128,1024]{2,1,0:T(8,128)(2,1)S(1)} %get-tuple-element.11.spread_ref, f32[96,384]{1,0:T(8,128)S(1)} %shard_map.58.own_ref, f32[96,384]{1,0:T(8,128)S(1)} %collective-permute-done.4.other_ref), custom_call_target="tpu_custom_call" | custom-call | tf_op jit(solution)/shard_map/pallas_call | solution.py:329
  36.2 11.9 %all_to_all.11.x_ref = bf16[16,80,128]{2,1,0:T(8,128)(2,1)S(1)} all-to-all(bf16[16,80,128]{2,1,0:T(8,128)(2,1)S(1)} %shard_map.60), channel_id=1, replica_groups={{26,28,30,0,2,4,6,8,10,12,14,16,18,20,22,24},{21,23,25,27,29,31,1,3,5,7..., dimensions={0} | all-to-all | bytes 655360 | tf_op jit(solution)/shard_map/all_to_all | solution.py:332
  48.1 0.0 copy-done
  48.1 1.3 %shard_map.61 = bf16[128,1280]{1,0:T(8,128)(2,1)} custom-call(bf16[16,80,128]{2,1,0:T(8,128)(2,1)S(1)} %all_to_all.11.x_ref, bf16[1280,1280]{1,0:T(8,128)(2,1)S(1)} %copy-done), custom_call_target="tpu_custom_call" | custom-call | tf_op jit(solution)/shard_map/pallas_call | solution.py:333
Async XLA Ops:
  0.0 23.0 %copy-start.1 = (s32[2,16]{1,0:T(2,128)S(1)}, s32[2,16]{1,0:T(2,128)}, u32[]{:S(2)}) copy-start(s32[2,16]{1,0:T(2,128)} %off_ref.5) | copy-start | bytes 388
  23.6 5.8 %collective-permute-start = (bf16[18,160,128]{2,1,0:T(8,128)(2,1)S(1)}, bf16[18,160,128]{2,1,0:T(8,128)(2,1)S(1)}, u32[]{:S(2)}, u32[]{:S(2)}) collective-permute-start(bf16[18,160,128]{2,1,0:T(8,128)(2,1)S(1)} %get-tuple-element.9.all_ref), channel_id=1, source_target_pairs={{0,1},{1,0},{2,3},{3,2},{4,5},{5,4},{6,7},{7,6},{8,9},{9,8},{10,11... | collective-permute-start | bytes 2211848 | tf_op jit(solution)/shard_map/ppermute | solution.py:310
  23.7 9.1 %collective-permute-start.1 = (bf16[400,128]{1,0:T(8,128)(2,1)S(1)}, bf16[400,128]{1,0:T(8,128)(2,1)S(1)}, u32[]{:S(2)}, u32[]{:S(2)}) collective-permute-start(bf16[400,128]{1,0:T(8,128)(2,1)S(1)} %get-tuple-element.12.refs_0_), channel_id=1, source_target_pairs={{0,32},{1,33},{2,34},{3,35},{4,36},{5,37},{6,38},{7,39},{8,40},{9,... | collective-permute-start | bytes 307208 | tf_op jit(solution)/shard_map/ppermute | solution.py:314
  25.2 8.1 %collective-permute-start.2 = (bf16[400,128]{1,0:T(8,128)(2,1)S(1)}, bf16[400,128]{1,0:T(8,128)(2,1)S(1)}, u32[]{:S(2)}, u32[]{:S(2)}) collective-permute-start(bf16[400,128]{1,0:T(8,128)(2,1)S(1)} %get-tuple-element.12.refs_0_), channel_id=1, source_target_pairs={{0,64},{1,65},{2,66},{3,67},{4,68},{5,69},{6,70},{7,71},{8,72},{9,... | collective-permute-start | bytes 307208 | tf_op jit(solution)/shard_map/ppermute | solution.py:314
  28.0 5.4 %collective-permute-start.3 = (bf16[400,128]{1,0:T(8,128)(2,1)S(1)}, bf16[400,128]{1,0:T(8,128)(2,1)S(1)}, u32[]{:S(2)}, u32[]{:S(2)}) collective-permute-start(bf16[400,128]{1,0:T(8,128)(2,1)S(1)} %get-tuple-element.12.refs_0_), channel_id=1, source_target_pairs={{0,96},{1,97},{2,98},{3,99},{4,100},{5,101},{6,102},{7,103},{8,104... | collective-permute-start | bytes 307208 | tf_op jit(solution)/shard_map/ppermute | solution.py:314
  34.2 13.9 %copy-start = (bf16[1280,1280]{1,0:T(8,128)(2,1)S(1)}, bf16[1280,1280]{1,0:T(8,128)(2,1)}, u32[]{:S(2)}) copy-start(bf16[1280,1280]{1,0:T(8,128)(2,1)} %w_ref.1) | copy-start | bytes 9830404
  34.2 1.5 %collective-permute-start.4 = (f32[96,384]{1,0:T(8,128)S(1)}, f32[96,384]{1,0:T(8,128)S(1)}, u32[]{:S(2)}, u32[]{:S(2)}) collective-permute-start(f32[96,384]{1,0:T(8,128)S(1)} %shard_map.59), channel_id=1, source_target_pairs={{0,1},{1,0},{2,3},{3,2},{4,5},{5,4},{6,7},{7,6},{8,9},{9,8},{10,11... | collective-permute-start | bytes 442376 | tf_op jit(solution)/shard_map/ppermute | solution.py:330
where the time goes:
time: 49.6 us; the launch traced here: 49.4 us
  blocking collectives  33.4 us (67%)
  Pallas kernels  8.86 us (18%)
  starting transfers between devices  5.89 us (12%)
  waiting for transfers between devices  1.13 us (2%)
    all_to_all x1, blocking collectives, on_device(): lax.all_to_all(packed, 'seq', 0, 0, axis_index_groups=planes[0], tiled=True)  21.5 us
    all_to_all x1, blocking collectives, on_device(): lax.all_to_all(mixed, 'seq', 0, 0, axis_index_groups=planes[1], tiled=True)  11.9 us
    ppermute x3, starting transfers between devices, on_device(): units.append(lax.ppermute(chosen, 'seq', pairs))  5.72 us
    pallas_call x1, Pallas kernels, on_device(): call(near_kernel, (shape(AUG, SEG1, dtype=F32), shape(3, 128, SEG1 // 2))...  3.35 us
    pallas_call x1, Pallas kernels, on_device(): call(pack_kernel, shape(HEADS, 3 * HDIM, ROWS), 0, 3, (pltpu.VMEM((3, ROW...  1.43 us
    pallas_call x1, Pallas kernels, on_device(): call(project_kernel, shape(ROWS, HEADS * HDIM), 2, scratch=(pltpu.VMEM((R...  1.32 us
  transfers between devices with their start and end apart: 5, of which 2 were waited for; matrix products, arithmetic and copies ran while one was open for 0% of the time, Pallas kernels for 8%

commit v1 on v0

--- a/solution.py
+++ b/solution.py
@@ -23,7 +23,7 @@
 SCALE = math.log2(math.e) / math.sqrt(HDIM)
 LOW = -1e30
 FLOOR = -1e9
-IN_ROOT = (14, 14)
+IN_ROOT = (13, 14)
 OUT_ROOT = (13, 10)
 BF = jnp.bfloat16
 F32 = jnp.float32

time: 49.6 us -> 49.7 us (level)
  no operation moved by 1% of the time
where the time goes in v1:
time: 49.7 us; the launch traced here: 49.5 us
  blocking collectives  33.4 us (67%)
  Pallas kernels  8.87 us (18%)
  starting transfers between devices  5.89 us (12%)
  waiting for transfers between devices  1.18 us (2%)
    all_to_all x1, blocking collectives, on_device(): lax.all_to_all(packed, 'seq', 0, 0, axis_index_groups=planes[0], tiled=True)  21.6 us
    all_to_all x1, blocking collectives, on_device(): lax.all_to_all(mixed, 'seq', 0, 0, axis_index_groups=planes[1], tiled=True)  11.8 us
    ppermute x3, starting transfers between devices, on_device(): units.append(lax.ppermute(chosen, 'seq', pairs))  5.72 us
    pallas_call x1, Pallas kernels, on_device(): call(near_kernel, (shape(AUG, SEG1, dtype=F32), shape(3, 128, SEG1 // 2))...  3.31 us
    pallas_call x1, Pallas kernels, on_device(): call(pack_kernel, shape(HEADS, 3 * HDIM, ROWS), 0, 3, (pltpu.VMEM((3, ROW...  1.44 us
    pallas_call x1, Pallas kernels, on_device(): call(project_kernel, shape(ROWS, HEADS * HDIM), 2, scratch=(pltpu.VMEM((R...  1.32 us
  transfers between devices with their start and end apart: 5, of which 2 were waited for; matrix products, arithmetic and copies ran while one was open for 0% of the time, Pallas kernels for 8%

profile of v1, /device:TPU:0, one launch (start us, length us, event | category | flops | bytes accessed | tf_op | source)
XLA Modules:
  0.0 49.5 jit_solution(1692298361891541342)
XLA Ops:
  0.0 0.0 copy-start.1
  0.0 1.4 %shard_map.55 = bf16[16,240,128]{2,1,0:T(8,128)(2,1)S(1)} custom-call(bf16[128,1280]{1,0:T(8,128)(2,1)} %q_hbm.1, bf16[128,1280]{1,0:T(8,128)(2,1)} %k_hbm.1, bf16[128,1280]{1,0:T(8,128)(2,1)} %v_hbm.1), custom_call_target="tpu_custom_call" | custom-call | tf_op jit(solution)/shard_map/pallas_call | solution.py:299
  1.4 21.6 %all_to_all.10.x_ref = bf16[16,240,128]{2,1,0:T(8,128)(2,1)S(1)} all-to-all(bf16[16,240,128]{2,1,0:T(8,128)(2,1)S(1)} %shard_map.55), channel_id=1, replica_groups={{26,28,30,0,2,4,6,8,10,12,14,16,18,20,22,24},{29,31,1,3,5,7,9,11,13,15,..., dimensions={0} | all-to-all | bytes 1966080 | tf_op jit(solution)/shard_map/all_to_all | solution.py:306
  23.1 0.0 copy-done.1
  23.1 0.6 %shard_map.56 = (bf16[400,128]{1,0:T(8,128)(2,1)S(1)}, bf16[18,160,128]{2,1,0:T(8,128)(2,1)S(1)}) custom-call(s32[2,16]{1,0:T(2,128)S(1)} %copy-done.1, bf16[16,240,128]{2,1,0:T(8,128)(2,1)S(1)} %all_to_all.10.x_ref), custom_call_target="tpu_custom_call" | custom-call | tf_op jit(solution)/shard_map/pallas_call | solution.py:307
  23.7 0.1 collective-permute-start
  23.8 1.6 %collective-permute-start.1 = (bf16[400,128]{1,0:T(8,128)(2,1)S(1)}, bf16[400,128]{1,0:T(8,128)(2,1)S(1)}, u32[]{:S(2)}, u32[]{:S(2)}) collective-permute-start(bf16[400,128]{1,0:T(8,128)(2,1)S(1)} %get-tuple-element.12.refs_0_), channel_id=1, source_target_pairs={{0,32},{1,33},{2,34},{3,35},{4,36},{5,37},{6,38},{7,39},{8,40},{9,... | collective-permute-start | bytes 307208 | tf_op jit(solution)/shard_map/ppermute | solution.py:314
  25.4 2.7 %collective-permute-start.2 = (bf16[400,128]{1,0:T(8,128)(2,1)S(1)}, bf16[400,128]{1,0:T(8,128)(2,1)S(1)}, u32[]{:S(2)}, u32[]{:S(2)}) collective-permute-start(bf16[400,128]{1,0:T(8,128)(2,1)S(1)} %get-tuple-element.12.refs_0_), channel_id=1, source_target_pairs={{0,64},{1,65},{2,66},{3,67},{4,68},{5,69},{6,70},{7,71},{8,72},{9,... | collective-permute-start | bytes 307208 | tf_op jit(solution)/shard_map/ppermute | solution.py:314
  28.1 1.4 %collective-permute-start.3 = (bf16[400,128]{1,0:T(8,128)(2,1)S(1)}, bf16[400,128]{1,0:T(8,128)(2,1)S(1)}, u32[]{:S(2)}, u32[]{:S(2)}) collective-permute-start(bf16[400,128]{1,0:T(8,128)(2,1)S(1)} %get-tuple-element.12.refs_0_), channel_id=1, source_target_pairs={{0,96},{1,97},{2,98},{3,99},{4,100},{5,101},{6,102},{7,103},{8,104... | collective-permute-start | bytes 307208 | tf_op jit(solution)/shard_map/ppermute | solution.py:314
  29.5 0.0 collective-permute-done.other_ref.all_ref
  29.5 3.3 %shard_map.57 = (f32[96,2048]{1,0:T(8,128)S(1)}, bf16[3,128,1024]{2,1,0:T(8,128)(2,1)S(1)}) custom-call(s32[2,16]{1,0:T(2,128)S(1)} %copy-done.1, bf16[16,240,128]{2,1,0:T(8,128)(2,1)S(1)} %all_to_all.10.x_ref, bf16[18,160,128]{2,1,0:T(8,128)(2,1)S(1)} %collective-permute-done.other_ref.all_ref), custom_call_target="tpu_custom_call" | custom-call | flops 6000000000 | bytes 10000000 | tf_op jit(solution)/shard_map/pallas_call | solution.py:315
  32.8 0.0 collective-permute-done.1.refs_1_
  32.9 0.6 %collective-permute-done.2.refs_2_ = bf16[400,128]{1,0:T(8,128)(2,1)S(1)} collective-permute-done((bf16[400,128]{1,0:T(8,128)(2,1)S(1)}, bf16[400,128]{1,0:T(8,128)(2,1)S(1)}, u32[]{:S(2)}, u32[]{:S(2)}) %collective-permute-start.2) | collective-permute-done | bytes 102432 | tf_op jit(solution)/shard_map/ppermute | solution.py:314
  33.5 0.0 collective-permute-done.3.refs_3_
  33.5 0.8 %shard_map.59 = f32[96,384]{1,0:T(8,128)S(1)} custom-call(bf16[18,160,128]{2,1,0:T(8,128)(2,1)S(1)} %collective-permute-done.other_ref.all_ref, bf16[400,128]{1,0:T(8,128)(2,1)S(1)} %get-tuple-element.12.refs_0_, bf16[400,128]{1,0:T(8,128)(2,1)S(1)} %collective-permute-done.1.refs_1_, bf16[400,128]{1,0:T(8,128)(2,1)S(1)} %collective-permute-done.2.refs_2_, ...), custom_call_target="tpu_custom_call" | custom-call | tf_op jit(solution)/shard_map/pallas_call | solution.py:322
  34.3 0.0 copy-start
  34.3 0.1 collective-permute-start.4
  34.4 0.8 %shard_map.58.own_ref = f32[96,384]{1,0:T(8,128)S(1)} custom-call(bf16[18,160,128]{2,1,0:T(8,128)(2,1)S(1)} %get-tuple-element.9.all_ref, bf16[400,128]{1,0:T(8,128)(2,1)S(1)} %get-tuple-element.12.refs_0_, bf16[400,128]{1,0:T(8,128)(2,1)S(1)} %collective-permute-done.1.refs_1_, bf16[400,128]{1,0:T(8,128)(2,1)S(1)} %collective-permute-done.2.refs_2_, ...), custom_call_target="tpu_custom_call" | custom-call | flops 1000000000 | bytes 10000000 | tf_op jit(solution)/shard_map/pallas_call | solution.py:323
  35.3 0.5 %collective-permute-done.4.other_ref = f32[96,384]{1,0:T(8,128)S(1)} collective-permute-done((f32[96,384]{1,0:T(8,128)S(1)}, f32[96,384]{1,0:T(8,128)S(1)}, u32[]{:S(2)}, u32[]{:S(2)}) %collective-permute-start.4) | collective-permute-done | bytes 147488 | tf_op jit(solution)/shard_map/ppermute | solution.py:330
  35.8 0.5 %shard_map.60 = bf16[16,80,128]{2,1,0:T(8,128)(2,1)S(1)} custom-call(s32[2,16]{1,0:T(2,128)S(1)} %copy-done.1, f32[96,2048]{1,0:T(8,128)S(1)} %get-tuple-element.10.refs_4_.state_ref, bf16[3,128,1024]{2,1,0:T(8,128)(2,1)S(1)} %get-tuple-element.11.spread_ref, f32[96,384]{1,0:T(8,128)S(1)} %shard_map.58.own_ref, f32[96,384]{1,0:T(8,128)S(1)} %collective-permute-done.4.other_ref), custom_call_target="tpu_custom_call" | custom-call | tf_op jit(solution)/shard_map/pallas_call | solution.py:329
  36.3 11.8 %all_to_all.11.x_ref = bf16[16,80,128]{2,1,0:T(8,128)(2,1)S(1)} all-to-all(bf16[16,80,128]{2,1,0:T(8,128)(2,1)S(1)} %shard_map.60), channel_id=1, replica_groups={{26,28,30,0,2,4,6,8,10,12,14,16,18,20,22,24},{21,23,25,27,29,31,1,3,5,7..., dimensions={0} | all-to-all | bytes 655360 | tf_op jit(solution)/shard_map/all_to_all | solution.py:332
  48.1 0.0 copy-done
  48.1 1.3 %shard_map.61 = bf16[128,1280]{1,0:T(8,128)(2,1)} custom-call(bf16[16,80,128]{2,1,0:T(8,128)(2,1)S(1)} %all_to_all.11.x_ref, bf16[1280,1280]{1,0:T(8,128)(2,1)S(1)} %copy-done), custom_call_target="tpu_custom_call" | custom-call | tf_op jit(solution)/shard_map/pallas_call | solution.py:333
Async XLA Ops:
  0.0 23.1 %copy-start.1 = (s32[2,16]{1,0:T(2,128)S(1)}, s32[2,16]{1,0:T(2,128)}, u32[]{:S(2)}) copy-start(s32[2,16]{1,0:T(2,128)} %off_ref.5) | copy-start | bytes 388
  23.7 5.8 %collective-permute-start = (bf16[18,160,128]{2,1,0:T(8,128)(2,1)S(1)}, bf16[18,160,128]{2,1,0:T(8,128)(2,1)S(1)}, u32[]{:S(2)}, u32[]{:S(2)}) collective-permute-start(bf16[18,160,128]{2,1,0:T(8,128)(2,1)S(1)} %get-tuple-element.9.all_ref), channel_id=1, source_target_pairs={{0,1},{1,0},{2,3},{3,2},{4,5},{5,4},{6,7},{7,6},{8,9},{9,8},{10,11... | collective-permute-start | bytes 2211848 | tf_op jit(solution)/shard_map/ppermute | solution.py:310
  23.8 9.0 %collective-permute-start.1 = (bf16[400,128]{1,0:T(8,128)(2,1)S(1)}, bf16[400,128]{1,0:T(8,128)(2,1)S(1)}, u32[]{:S(2)}, u32[]{:S(2)}) collective-permute-start(bf16[400,128]{1,0:T(8,128)(2,1)S(1)} %get-tuple-element.12.refs_0_), channel_id=1, source_target_pairs={{0,32},{1,33},{2,34},{3,35},{4,36},{5,37},{6,38},{7,39},{8,40},{9,... | collective-permute-start | bytes 307208 | tf_op jit(solution)/shard_map/ppermute | solution.py:314
  25.4 8.1 %collective-permute-start.2 = (bf16[400,128]{1,0:T(8,128)(2,1)S(1)}, bf16[400,128]{1,0:T(8,128)(2,1)S(1)}, u32[]{:S(2)}, u32[]{:S(2)}) collective-permute-start(bf16[400,128]{1,0:T(8,128)(2,1)S(1)} %get-tuple-element.12.refs_0_), channel_id=1, source_target_pairs={{0,64},{1,65},{2,66},{3,67},{4,68},{5,69},{6,70},{7,71},{8,72},{9,... | collective-permute-start | bytes 307208 | tf_op jit(solution)/shard_map/ppermute | solution.py:314
  28.1 5.4 %collective-permute-start.3 = (bf16[400,128]{1,0:T(8,128)(2,1)S(1)}, bf16[400,128]{1,0:T(8,128)(2,1)S(1)}, u32[]{:S(2)}, u32[]{:S(2)}) collective-permute-start(bf16[400,128]{1,0:T(8,128)(2,1)S(1)} %get-tuple-element.12.refs_0_), channel_id=1, source_target_pairs={{0,96},{1,97},{2,98},{3,99},{4,100},{5,101},{6,102},{7,103},{8,104... | collective-permute-start | bytes 307208 | tf_op jit(solution)/shard_map/ppermute | solution.py:314
  34.3 13.8 %copy-start = (bf16[1280,1280]{1,0:T(8,128)(2,1)S(1)}, bf16[1280,1280]{1,0:T(8,128)(2,1)}, u32[]{:S(2)}) copy-start(bf16[1280,1280]{1,0:T(8,128)(2,1)} %w_ref.1) | copy-start | bytes 9830404
  34.3 1.5 %collective-permute-start.4 = (f32[96,384]{1,0:T(8,128)S(1)}, f32[96,384]{1,0:T(8,128)S(1)}, u32[]{:S(2)}, u32[]{:S(2)}) collective-permute-start(f32[96,384]{1,0:T(8,128)S(1)} %shard_map.59), channel_id=1, source_target_pairs={{0,1},{1,0},{2,3},{3,2},{4,5},{5,4},{6,7},{7,6},{8,9},{9,8},{10,11... | collective-permute-start | bytes 442376 | tf_op jit(solution)/shard_map/ppermute | solution.py:330
